TPU v7x, 256 devices: a whole 4x4x8 slice. The times are simulated.
256 devices in a mesh: dp: 64 (over y, x, z_hi), tensor: 4 (over z_lo, core).
Axes of the slice: x: 4, y: 4, z: 8 (z_hi: 4, z_lo: 2; z = z_hi * 2 + z_lo), core: 2. Of those that a mesh axis runs over, the one named last changes fastest.
Arguments:
- layer_inputs: bfloat16 [32768, 4096], P('dp', 'tensor'), may hold values from -6 to 6
- gate_pre: bfloat16 [32768, 14336], P('dp', 'tensor'), may hold values from -6 to 6
- up_pre: bfloat16 [32768, 14336], P('dp', 'tensor'), may hold values from -6 to 6
- hidden_grad: bfloat16 [32768, 14336], P('dp', 'tensor'), may hold values from -6 to 6
- output_grad: bfloat16 [32768, 4096], P('dp', 'tensor'), may hold values from -6 to 6
- proj_in: bfloat16 [4096, 64], replicated, may hold values from -0.09375 to 0.09375
- proj_out: bfloat16 [4096, 64], replicated, may hold values from -0.09375 to 0.09375
- proj_gate: bfloat16 [14336, 64], P('tensor'), may hold values from -0.046875 to 0.046875
- proj_up: bfloat16 [14336, 64], P('tensor'), may hold values from -0.046875 to 0.046875
- proj_hidden: bfloat16 [14336, 64], P('tensor'), may hold values from -0.046875 to 0.046875
- query_grads: bfloat16 [128, 3, 64, 64], P('dp'), may hold values from -6 to 6
Outputs:
- scores: float32 [128, 64], P(None, 'dp')
All inputs are finite; a program needn't handle non-finite values.
Results may differ from a plain program's by a relative error of at most 0.0053.
Values may be sent and summed in bfloat16 or wider, within the bound.
No kernel may reach another device: no remote copies, remote signals or barrier semaphores. Data moves between devices by JAX's collectives and lax.ppermute only.
A program may use at most 128 MiB of HBM per device.

v0:
```python
import jax
import jax.numpy as jnp
from jax import lax
from jax.experimental import pallas as pl
from jax.experimental.pallas import tpu as pltpu
from jax.sharding import PartitionSpec as P

HIGH = lax.Precision.HIGHEST
DAMP = 0.1
RANK = 64
WIDE = 2 * RANK
STRIP = 128
AHEAD = 3
SIDE = 4
VMEM_BYTES = 32 * 1024 * 1024

TERMS = 3
PACKED = RANK // 2 + 16
FACTOR_ROWS = TERMS * PACKED
SMALL_VMEM = 32 * 1024 * 1024
RINGS = {"y": 16, "x": 4, "z": 1}


def layer_of(tensor_at):
    return jnp.minimum(tensor_at, 2)


def rows_dot(a, b):
    return lax.dot_general(a, b, (((1,), (1,)), ((), ())), preferred_element_type=jnp.float32)


def project_kernel(
    gate_hbm, up_hbm, grad_hbm, inputs_hbm, outg_hbm,
    win_hbm, wout_hbm, wgate_hbm, wup_hbm, whid_hbm, query_hbm,
    own_ref, core_ref, pieces_ref,
    hidden_buf, side_buf, hidden_w, side_w, query_buf, sums, sems, side_sems,
):
    tensor_at = lax.axis_index("tensor")
    tokens, hidden = gate_hbm.shape
    features = inputs_hbm.shape[1]
    strips = tokens // STRIP

    def weight_copies():
        mine = pl.ds(pl.multiple_of(tensor_at * features, features), features)
        return [
            pltpu.make_async_copy(src.at[:, mine], side_w.at[i], side_sems.at[2 + i])
            for i, src in enumerate((win_hbm, wout_hbm))
        ] + [
            pltpu.make_async_copy(src, hidden_w.at[i], side_sems.at[5 + i])
            for i, src in enumerate((wgate_hbm, wup_hbm, whid_hbm))
        ]

    def chunk_copies(c):
        rows = pl.ds(pl.multiple_of(c * STRIP, STRIP), STRIP)
        return [
            pltpu.make_async_copy(src.at[rows, :], hidden_buf.at[i, rows, :], sems.at[i, c])
            for i, src in enumerate((gate_hbm, up_hbm, grad_hbm))
        ] + [
            pltpu.make_async_copy(src.at[rows, :], side_buf.at[i, rows, :], sems.at[3 + i, c])
            for i, src in enumerate((inputs_hbm, outg_hbm))
        ]

    def start(copies):
        for copy in copies:
            copy.start()

    def arrive(copies):
        for copy in copies:
            copy.wait()

    query_copy = pltpu.make_async_copy(query_hbm, query_buf, side_sems.at[4])
    query_copy.start()
    start(weight_copies())
    start(chunk_copies(0))

    @pl.loop(0, strips)
    def _(c):
        arrive(chunk_copies(c))

        @pl.when(c == 0)
        def _():
            for k in range(1, 3):
                start(chunk_copies(k))
            arrive(weight_copies())

        @pl.when((c > 0) & (c + 2 < strips))
        def _():
            start(chunk_copies(c + 2))

        at = pl.ds(pl.multiple_of(c * STRIP, STRIP), STRIP)
        g = hidden_buf[0, at, :].astype(jnp.float32)
        u = hidden_buf[1, at, :].astype(jnp.float32)
        e = hidden_buf[2, at, :].astype(jnp.float32)
        th = jnp.tanh(0.5 * g)
        p, q = 1.0 + th, 1.0 - th
        a = g * p
        gate_grad = ((e * u) * (p * (2.0 + g * q))).astype(jnp.bfloat16)
        up_grad = (e * a).astype(jnp.bfloat16)
        hid = (a * u).astype(jnp.bfloat16)
        for i, act in enumerate((gate_grad, up_grad, hid)):
            sums[i, at, :RANK] = rows_dot(act, hidden_w[i]) * (0.25 if i == 0 else 0.5)
        for i in range(2):
            sums[2 * i, at, RANK:] = rows_dot(side_buf[i, at, :], side_w[i])

    query_copy.wait()
    layer = layer_of(tensor_at)
    for q in range(2):
        rows = query_buf[q, layer].astype(jnp.float32)
        rows = jnp.where(layer == 2, rows.T, rows)
        packed = jnp.concatenate([rows[: RANK // 2], rows[RANK // 2 :]], axis=1)
        pieces_ref[q * (RANK // 2) : (q + 1) * (RANK // 2), :] = packed.astype(jnp.bfloat16)

    sums[1, :, RANK:] = sums[0, :, RANK:]
    core = tensor_at & 1
    core_ref[:tokens, :] = sums[1 - core].astype(jnp.bfloat16)
    core_ref[tokens:, :] = sums[2].astype(jnp.bfloat16)
    own_ref[:tokens, :] = sums[core]
    own_ref[tokens:, :] = sums[2]


def project(gate_pre, up_pre, hidden_grad, layer_inputs, output_grad, proj_in, proj_out, proj_gate, proj_up, proj_hidden, query_grads):
    tokens, hidden = gate_pre.shape
    features = layer_inputs.shape[1]
    inside = pl.BlockSpec(memory_space=pltpu.VMEM)
    buf = lambda *shape: pltpu.VMEM(shape, jnp.bfloat16)
    flops = 2 * tokens * (3 * hidden + 2 * features) * RANK
    return pl.pallas_call(
        project_kernel,
        out_shape=[
            jax.ShapeDtypeStruct((2 * tokens, WIDE), jnp.float32),
            jax.ShapeDtypeStruct((2 * tokens, WIDE), jnp.bfloat16),
            jax.ShapeDtypeStruct((RANK, WIDE), jnp.bfloat16),
        ],
        in_specs=[pl.BlockSpec(memory_space=pltpu.HBM)] * 11,
        out_specs=[inside] * 3,
        scratch_shapes=[
            buf(3, tokens, hidden),
            buf(2, tokens, features),
            buf(3, RANK, hidden),
            buf(2, RANK, features),
            buf(*query_grads.shape),
            pltpu.VMEM((3, tokens, WIDE), jnp.float32),
            pltpu.SemaphoreType.DMA((5, tokens // STRIP)),
            pltpu.SemaphoreType.DMA((8,)),
        ],
        compiler_params=pltpu.CompilerParams(vmem_limit_bytes=VMEM_BYTES),
        cost_estimate=pl.CostEstimate(flops=flops, bytes_accessed=17_000_000, transcendentals=tokens * hidden),
        name="project",
    )(gate_pre, up_pre, hidden_grad, layer_inputs, output_grad, *[pltpu.with_memory_space_constraint(v, pltpu.HBM) for v in (proj_in.T, proj_out.T, proj_gate.T, proj_up.T, proj_hidden.T, query_grads)])


def square_iota(axis):
    return lax.broadcasted_iota(jnp.int32, (RANK, RANK), axis)


def pack(a, b):
    row, col = square_iota(0), square_iota(1)
    both = jnp.where(row >= col, a, b)
    diag = jnp.where(row == col, b, 0.0).sum(axis=0, keepdims=True)
    diag = jnp.broadcast_to(jnp.concatenate([diag, diag], axis=1), (PACKED - RANK // 2, WIDE))
    return jnp.concatenate([jnp.concatenate([both[: RANK // 2], both[RANK // 2 :]], axis=1), diag], axis=0)


def unpack(packed):
    row, col = square_iota(0), square_iota(1)
    half = packed[: RANK // 2]
    both = jnp.concatenate([half[:, :RANK], half[:, RANK:]], axis=0)
    diag = packed[RANK // 2 : RANK // 2 + 1, :RANK]
    a = jnp.where(row >= col, both, both.T)
    b = jnp.where(row < col, both, jnp.where(row == col, diag, both.T))
    return jnp.concatenate([a, b], axis=1)


def put_sum(out_ref, value):
    for i in range(TERMS):
        term = value.astype(jnp.bfloat16)
        out_ref[i * PACKED : (i + 1) * PACKED, :] = term
        value = value - term.astype(jnp.float32)


def get_sum(ref):
    terms = [ref[i * PACKED : (i + 1) * PACKED, :].astype(jnp.float32) for i in range(TERMS)]
    return (terms[2] + terms[1]) + terms[0]


def total_of(refs):
    parts = [get_sum(ref) for ref in refs]
    while len(parts) > 1:
        parts = [a + b for a, b in zip(parts[::2], parts[1::2])]
    return parts[0]


def chip_kernel(own_ref, core_ref, keep_ref, send_ref):
    tokens = keep_ref.shape[0]
    far = lax.shift_right_logical(lax.axis_index("tensor"), 1)
    kept, sent = [pl.ds(pl.multiple_of(at * tokens, tokens), tokens) for at in (far, 1 - far)]
    keep_ref[...] = own_ref[kept, :] + core_ref[kept, :].astype(jnp.float32)
    send_ref[...] = (own_ref[sent, :] + core_ref[sent, :].astype(jnp.float32)).astype(jnp.bfloat16)


def chip_sums(own, core):
    inside = pl.BlockSpec(memory_space=pltpu.VMEM)
    shape = (own.shape[0] // 2, own.shape[1])
    return pl.pallas_call(
        chip_kernel,
        out_shape=[jax.ShapeDtypeStruct(shape, jnp.float32), jax.ShapeDtypeStruct(shape, jnp.bfloat16)],
        in_specs=[inside] * 2,
        out_specs=[inside] * 2,
        compiler_params=pltpu.CompilerParams(vmem_limit_bytes=SMALL_VMEM),
        name="chip_sums",
    )(own, core)


def gram_kernel(keep_ref, got_ref, pieces_ref, message_ref, cross_ref):
    f32 = jnp.float32
    v = keep_ref[...] + got_ref[...].astype(f32)
    m = lax.dot_general(v, v, (((0,), (0,)), ((), ())), precision=HIGH, preferred_element_type=f32)
    left = lax.broadcasted_iota(jnp.int32, (RANK, WIDE), 1) < RANK
    put_sum(message_ref, pack(m[:RANK, :RANK], m[RANK:, RANK:]))
    message_ref[FACTOR_ROWS:, :] = pieces_ref[...]
    cross_ref[...] = jnp.where(left, m[RANK:], m[:RANK])


def gram(parts, pieces):
    inside = pl.BlockSpec(memory_space=pltpu.VMEM)
    return pl.pallas_call(
        gram_kernel,
        out_shape=[
            jax.ShapeDtypeStruct((FACTOR_ROWS + pieces.shape[0], WIDE), jnp.bfloat16),
            jax.ShapeDtypeStruct((RANK, WIDE), jnp.float32),
        ],
        in_specs=[inside] * 3,
        out_specs=[inside] * 2,
        compiler_params=pltpu.CompilerParams(vmem_limit_bytes=SMALL_VMEM),
        name="gram",
    )(*parts, pieces)


def merge_kernel(*refs):
    parts, out_ref = refs[:-1], refs[-1]
    put_sum(out_ref, total_of(parts))
    rows = parts[0].shape[0] - FACTOR_ROWS
    for i, ref in enumerate(parts):
        out_ref[FACTOR_ROWS + i * rows : FACTOR_ROWS + (i + 1) * rows, :] = ref[FACTOR_ROWS:, :]


def merge(parts):
    inside = pl.BlockSpec(memory_space=pltpu.VMEM)
    rows = FACTOR_ROWS + len(parts) * (parts[0].shape[0] - FACTOR_ROWS)
    return pl.pallas_call(
        merge_kernel,
        out_shape=jax.ShapeDtypeStruct((rows, WIDE), jnp.bfloat16),
        in_specs=[inside] * len(parts),
        out_specs=inside,
        compiler_params=pltpu.CompilerParams(vmem_limit_bytes=SMALL_VMEM),
        name="merge",
    )(*parts)


def solve_two(m, rows):
    (a, b), (c, d) = m
    scale = 1.0 / (a * d - b * c)
    a, b, c, d = d * scale, b * scale, c * scale, a * scale
    return a * rows[0] - b * rows[1], d * rows[1] - c * rows[0]


def invert_pair(w):
    lane = lax.broadcasted_iota(jnp.int32, (RANK, WIDE), 1)
    row_at = lax.broadcasted_iota(jnp.int32, (RANK, WIDE), 0)
    left = lane < RANK
    column_at = jnp.where(left, lane, lane - RANK)

    def column(k):
        return jnp.where(
            left,
            jnp.broadcast_to(w[:, k : k + 1], (RANK, WIDE)),
            jnp.broadcast_to(w[:, RANK + k : RANK + k + 1], (RANK, WIDE)),
        )

    for k in range(0, RANK, 4):
        cols = [column(k + i) for i in range(4)]
        m = [[c[k + i : k + i + 1] for c in cols] for i in range(4)]
        at = column_at[:1]
        rows = [
            jnp.where((at >= k) & (at < k + 4), jnp.where(at == k + i, 1.0, 0.0), w[k + i : k + i + 1])
            for i in range(4)
        ]
        upper = [m[0][:2], m[1][:2]]
        x0, x1 = solve_two(upper, rows[:2])
        e02, e12 = solve_two(upper, (m[0][2], m[1][2]))
        e03, e13 = solve_two(upper, (m[0][3], m[1][3]))
        rest = [[m[i][2] - m[i][0] * e02 - m[i][1] * e12, m[i][3] - m[i][0] * e03 - m[i][1] * e13] for i in (2, 3)]
        n2, n3 = solve_two(rest, [rows[i] - m[i][0] * x0 - m[i][1] * x1 for i in (2, 3)])
        new = [x0 - e02 * n2 - e03 * n3, x1 - e12 * n2 - e13 * n3, n2, n3]
        out = jnp.where((column_at >= k) & (column_at < k + 4), 0.0, w)
        out = (out - cols[0] * new[0] - cols[1] * new[1]) - (cols[2] * new[2] + cols[3] * new[3])
        for i in range(4):
            out = jnp.where(row_at == k + i, new[i], out)
        w = out
    return w


def score_kernel(count, cross_ref, *refs):
    parts, out_ref = refs[:-1], refs[-1]
    f32 = jnp.float32
    lane = lax.broadcasted_iota(jnp.int32, (RANK, WIDE), 1)
    row_at = lax.broadcasted_iota(jnp.int32, (RANK, WIDE), 0)
    diag = (lane == row_at) | (lane == row_at + RANK)
    inv = invert_pair(unpack(total_of(parts)) * (1.0 / count) + jnp.where(diag, DAMP, 0.0))
    dot = lambda a, b: jnp.dot(a, b, precision=HIGH, preferred_element_type=f32)
    h = dot(dot(inv[:, :RANK], cross_ref[:, RANK:]), inv[:, RANK:])
    h = jnp.concatenate([h[: RANK // 2], h[RANK // 2 :]], axis=1).reshape(1, SIDE, 8, WIDE)
    sums = []
    for ref in parts:
        q = ref[FACTOR_ROWS:, :].astype(f32)
        q = q.reshape(q.shape[0] // (RANK // 2), SIDE, 8, WIDE)
        sums.append((q * h).sum(axis=1).sum(axis=1))
    sums = jnp.concatenate(sums, axis=0)
    queries = sums.shape[0]
    me = lax.axis_index("dp")
    j = lax.broadcasted_iota(jnp.int32, (queries, queries), 0)
    want = lax.broadcasted_iota(jnp.int32, (queries, queries), 1)
    last, middle = lax.shift_right_logical(j, 5), lax.shift_right_logical(j, 3)
    swap = (lax.axis_index("tensor") & 1) == 1
    y = (lax.shift_right_logical(me, 4) - jnp.where(swap, middle, last)) & 3
    x = (lax.shift_right_logical(me, 2) - jnp.where(swap, last, middle)) & 3
    step = lax.shift_right_logical(j, 1) & 3
    z = (me & 3) ^ step ^ lax.shift_right_logical(step, 1)
    source = y * 32 + x * 8 + z * 2 + (j & 1)
    place = jnp.where(source == want, 1.0, 0.0).astype(f32)
    by_row = sums.sum(axis=1, keepdims=True) * (1.0 / (RANK * RANK))
    row = (place * by_row).sum(axis=0, keepdims=True)
    out_ref[...] = jnp.where(lax.axis_index("tensor") == 3, 0.0, row)


def score(count, cross, parts):
    inside = pl.BlockSpec(memory_space=pltpu.VMEM)
    total = sum(p.shape[0] - FACTOR_ROWS for p in parts) // (RANK // 2)
    return pl.pallas_call(
        lambda *refs: score_kernel(count, *refs),
        out_shape=jax.ShapeDtypeStruct((1, total), jnp.float32),
        in_specs=[inside] * (1 + SIDE),
        out_specs=inside,
        compiler_params=pltpu.CompilerParams(vmem_limit_bytes=SMALL_VMEM),
        name="score",
    )(cross, *parts)


def ring(names, step, size):
    def to(i, t):
        stride = RINGS[names[t & 1]]
        at = (i // stride) % SIDE
        return (i + ((at + step) % SIDE - at) * stride) * 4 + t

    return [(i * 4 + t, to(i, t)) for i in range(size) for t in range(4)]


def flipped(stride, mask, size):
    def to(i):
        at = (i // stride) % SIDE
        return i + ((at ^ mask) - at) * stride

    return [(i, to(i)) for i in range(size)]


def body(
    layer_inputs, gate_pre, up_pre, hidden_grad, output_grad,
    proj_in, proj_out, proj_gate, proj_up, proj_hidden, query_grads,
):
    size = lax.axis_size("dp")

    def around(value, names):
        far, near, back = [lax.ppermute(value, ("dp", "tensor"), ring(names, s, size)) for s in (2, 1, 3)]
        return [value, near, far, back]

    def crossed(value, mask):
        return lax.ppermute(value, "tensor", [(i, i ^ mask) for i in range(4)])

    def shifted(value, step):
        return lax.ppermute(value, "tensor", [(i, (i + step) % 4) for i in range(4)])

    stay = lambda v: pltpu.with_memory_space_constraint(v, pltpu.HBM)
    gate_pre, up_pre, hidden_grad, layer_inputs, output_grad = map(stay, (gate_pre, up_pre, hidden_grad, layer_inputs, output_grad))
    own, other, pieces = project(
        gate_pre, up_pre, hidden_grad, layer_inputs, output_grad,
        proj_in, proj_out, proj_gate, proj_up, proj_hidden, query_grads,
    )
    keep, send = chip_sums(own, crossed(other, 1))
    message, cross = gram((keep, crossed(send, 2)), pieces)
    for mask in (1, 3):
        message = merge([message, lax.ppermute(message, "dp", flipped(RINGS["z"], mask, size))])
    message = merge(around(message, "xy"))
    part = score(layer_inputs.shape[0] * size, cross, around(message, "yx"))
    parts = [part] + [shifted(part, s) for s in (1, 2, 3)]
    at = lax.axis_index("tensor")

    def of(index):
        picked = parts[3]
        for s in (2, 1, 0):
            picked = jnp.where((at - index) % 4 == s, parts[s], picked)
        return picked

    return ((of(0) + of(1)) + of(2)).reshape(-1, 1)


def solution(mesh):
    placed = (
        P("dp", "tensor"), P("dp", "tensor"), P("dp", "tensor"), P("dp", "tensor"), P("dp", "tensor"),
        P(), P(), P("tensor", None), P("tensor", None), P("tensor", None),
        P("dp", None, None, None),
    )
    return jax.shard_map(body, mesh=mesh, in_specs=placed, out_specs=P(None, "dp"), check_vma=False)
```

profile of v0, /device:TPU:1, one launch (start us, length us, event | category | flops | bytes accessed | tf_op | source)
XLA Modules:
  0.0 63.4 jit_solution(16184847836994339443)
XLA Ops:
  0.0 9.4 %project.1 = (f32[1024,128]{1,0:T(8,128)S(1)}, bf16[1024,128]{1,0:T(8,128)(2,1)S(1)}, bf16[64,128]{1,0:T(8,128)(2,1)S(1)}) custom-call(bf16[512,3584]{1,0:T(8,128)(2,1)} %gate_hbm.1, bf16[512,3584]{1,0:T(8,128)(2,1)} %up_hbm.1, bf16[512,3584]{1,0:T(8,128)(2,1)} %grad_hbm.1, bf16[512,1024]{1,0:T(8,128)(2,1)} %inputs_hbm.1, bf16[512,1024]{1,0:T(8,128)(2,1)} %outg_hbm.1, ...), custom_call_target="tpu_custom_call" | custom-call | flops 838860800 | bytes 17000000 | tf_op jit(solution)/shard_map/project/pallas_call | solution.py:127
  9.4 3.3 %collective-permute-start = (bf16[1024,128]{1,0:T(8,128)(2,1)S(1)}, bf16[1024,128]{1,0:T(8,128)(2,1)S(1)}, u32[]{:S(2)}, u32[]{:S(2)}) collective-permute-start(bf16[1024,128]{1,0:T(8,128)(2,1)S(1)} %get-tuple-element.13), channel_id=1, source_target_pairs={{0,1},{1,0},{2,3},{3,2},{4,5},{5,4},{6,7},{7,6},{8,9},{9,8},{10,11... | collective-permute-start | bytes 786440 | tf_op jit(solution)/shard_map/ppermute | solution.py:377
  12.7 1.2 %collective-permute-done.core_ref = bf16[1024,128]{1,0:T(8,128)(2,1)S(1)} collective-permute-done((bf16[1024,128]{1,0:T(8,128)(2,1)S(1)}, bf16[1024,128]{1,0:T(8,128)(2,1)S(1)}, u32[]{:S(2)}, u32[]{:S(2)}) %collective-permute-start) | collective-permute-done | bytes 262176 | tf_op jit(solution)/shard_map/ppermute | solution.py:377
  13.9 0.1 collective-permute-start.1
  14.0 4.7 %collective-permute-done.1.got_ref = bf16[512,128]{1,0:T(8,128)(2,1)S(1)} collective-permute-done((bf16[512,128]{1,0:T(8,128)(2,1)S(1)}, bf16[512,128]{1,0:T(8,128)(2,1)S(1)}, u32[]{:S(2)}, u32[]{:S(2)}) %collective-permute-start.1) | collective-permute-done | bytes 131104 | tf_op jit(solution)/shard_map/ppermute | solution.py:377
  18.7 0.6 gram.1
  19.3 1.7 %collective-permute-start.2 = (bf16[208,128]{1,0:T(8,128)(2,1)S(1)}, bf16[208,128]{1,0:T(8,128)(2,1)S(1)}, u32[]{:S(2)}, u32[]{:S(2)}) collective-permute-start(bf16[208,128]{1,0:T(8,128)(2,1)S(1)} %get-tuple-element.18.refs_0_), channel_id=1, source_target_pairs={{0,4},{4,0},{8,12},{12,8},{16,20},{20,16},{24,28},{28,24},{32,36},... | collective-permute-start | bytes 159752 | tf_op jit(solution)/shard_map/ppermute | solution.py:391
  21.0 2.8 %collective-permute-done.2.refs_1_ = bf16[208,128]{1,0:T(8,128)(2,1)S(1)} collective-permute-done((bf16[208,128]{1,0:T(8,128)(2,1)S(1)}, bf16[208,128]{1,0:T(8,128)(2,1)S(1)}, u32[]{:S(2)}, u32[]{:S(2)}) %collective-permute-start.2) | collective-permute-done | bytes 53280 | tf_op jit(solution)/shard_map/ppermute | solution.py:391
  23.9 3.9 %collective-permute-start.3 = (bf16[272,128]{1,0:T(8,128)(2,1)S(1)}, bf16[272,128]{1,0:T(8,128)(2,1)S(1)}, u32[]{:S(2)}, u32[]{:S(2)}) collective-permute-start(bf16[272,128]{1,0:T(8,128)(2,1)S(1)} %merge.3.refs_0_), channel_id=1, source_target_pairs={{0,12},{4,8},{8,4},{12,0},{16,28},{20,24},{24,20},{28,16},{32,44},... | collective-permute-start | bytes 208904 | tf_op jit(solution)/shard_map/ppermute | solution.py:391
  27.8 1.8 %collective-permute-done.3.refs_1_ = bf16[272,128]{1,0:T(8,128)(2,1)S(1)} collective-permute-done((bf16[272,128]{1,0:T(8,128)(2,1)S(1)}, bf16[272,128]{1,0:T(8,128)(2,1)S(1)}, u32[]{:S(2)}, u32[]{:S(2)}) %collective-permute-start.3) | collective-permute-done | bytes 69664 | tf_op jit(solution)/shard_map/ppermute | solution.py:391
  29.6 1.4 %collective-permute-start.4 = (bf16[400,128]{1,0:T(8,128)(2,1)S(1)}, bf16[400,128]{1,0:T(8,128)(2,1)S(1)}, u32[]{:S(2)}, u32[]{:S(2)}) collective-permute-start(bf16[400,128]{1,0:T(8,128)(2,1)S(1)} %merge.4.refs_0_), channel_id=1, source_target_pairs={{0,16},{1,65},{2,18},{3,67},{4,20},{5,69},{6,22},{7,71},{8,24},{9,... | collective-permute-start | bytes 307208 | tf_op jit(solution)/shard_map/ppermute | solution.py:373
  31.0 2.6 %collective-permute-start.5 = (bf16[400,128]{1,0:T(8,128)(2,1)S(1)}, bf16[400,128]{1,0:T(8,128)(2,1)S(1)}, u32[]{:S(2)}, u32[]{:S(2)}) collective-permute-start(bf16[400,128]{1,0:T(8,128)(2,1)S(1)} %merge.4.refs_0_), channel_id=1, source_target_pairs={{0,32},{1,129},{2,34},{3,131},{4,36},{5,133},{6,38},{7,135},{8,40}... | collective-permute-start | bytes 307208 | tf_op jit(solution)/shard_map/ppermute | solution.py:373
  33.6 1.1 %collective-permute-start.6 = (bf16[400,128]{1,0:T(8,128)(2,1)S(1)}, bf16[400,128]{1,0:T(8,128)(2,1)S(1)}, u32[]{:S(2)}, u32[]{:S(2)}) collective-permute-start(bf16[400,128]{1,0:T(8,128)(2,1)S(1)} %merge.4.refs_0_), channel_id=1, source_target_pairs={{0,48},{1,193},{2,50},{3,195},{4,52},{5,197},{6,54},{7,199},{8,56}... | collective-permute-start | bytes 307208 | tf_op jit(solution)/shard_map/ppermute | solution.py:373
  34.6 0.0 collective-permute-done.4.refs_1_
  34.6 2.1 %collective-permute-done.5.refs_2_ = bf16[400,128]{1,0:T(8,128)(2,1)S(1)} collective-permute-done((bf16[400,128]{1,0:T(8,128)(2,1)S(1)}, bf16[400,128]{1,0:T(8,128)(2,1)S(1)}, u32[]{:S(2)}, u32[]{:S(2)}) %collective-permute-start.5) | collective-permute-done | bytes 102432 | tf_op jit(solution)/shard_map/ppermute | solution.py:373
  36.7 0.7 %collective-permute-done.6.refs_3_ = bf16[400,128]{1,0:T(8,128)(2,1)S(1)} collective-permute-done((bf16[400,128]{1,0:T(8,128)(2,1)S(1)}, bf16[400,128]{1,0:T(8,128)(2,1)S(1)}, u32[]{:S(2)}, u32[]{:S(2)}) %collective-permute-start.6) | collective-permute-done | bytes 102432 | tf_op jit(solution)/shard_map/ppermute | solution.py:373
  37.4 1.0 %collective-permute-start.7 = (bf16[1168,128]{1,0:T(8,128)(2,1)S(1)}, bf16[1168,128]{1,0:T(8,128)(2,1)S(1)}, u32[]{:S(2)}, u32[]{:S(2)}) collective-permute-start(bf16[1168,128]{1,0:T(8,128)(2,1)S(1)} %merge.5.refs_1_), channel_id=1, source_target_pairs={{0,64},{1,17},{2,66},{3,19},{4,68},{5,21},{6,70},{7,23},{8,72},{9,... | collective-permute-start | bytes 897032 | tf_op jit(solution)/shard_map/ppermute | solution.py:373
  38.5 2.4 %collective-permute-start.8 = (bf16[1168,128]{1,0:T(8,128)(2,1)S(1)}, bf16[1168,128]{1,0:T(8,128)(2,1)S(1)}, u32[]{:S(2)}, u32[]{:S(2)}) collective-permute-start(bf16[1168,128]{1,0:T(8,128)(2,1)S(1)} %merge.5.refs_1_), channel_id=1, source_target_pairs={{0,128},{1,33},{2,130},{3,35},{4,132},{5,37},{6,134},{7,39},{8,136... | collective-permute-start | bytes 897032 | tf_op jit(solution)/shard_map/ppermute | solution.py:373
  40.9 1.2 %collective-permute-start.9 = (bf16[1168,128]{1,0:T(8,128)(2,1)S(1)}, bf16[1168,128]{1,0:T(8,128)(2,1)S(1)}, u32[]{:S(2)}, u32[]{:S(2)}) collective-permute-start(bf16[1168,128]{1,0:T(8,128)(2,1)S(1)} %merge.5.refs_1_), channel_id=1, source_target_pairs={{0,192},{1,49},{2,194},{3,51},{4,196},{5,53},{6,198},{7,55},{8,200... | collective-permute-start | bytes 897032 | tf_op jit(solution)/shard_map/ppermute | solution.py:373
  42.1 2.3 %collective-permute-done.7.refs_2_ = bf16[1168,128]{1,0:T(8,128)(2,1)S(1)} collective-permute-done((bf16[1168,128]{1,0:T(8,128)(2,1)S(1)}, bf16[1168,128]{1,0:T(8,128)(2,1)S(1)}, u32[]{:S(2)}, u32[]{:S(2)}) %collective-permute-start.7) | collective-permute-done | bytes 299040 | tf_op jit(solution)/shard_map/ppermute | solution.py:373
  44.3 3.9 %collective-permute-done.8.refs_3_ = bf16[1168,128]{1,0:T(8,128)(2,1)S(1)} collective-permute-done((bf16[1168,128]{1,0:T(8,128)(2,1)S(1)}, bf16[1168,128]{1,0:T(8,128)(2,1)S(1)}, u32[]{:S(2)}, u32[]{:S(2)}) %collective-permute-start.8) | collective-permute-done | bytes 299040 | tf_op jit(solution)/shard_map/ppermute | solution.py:373
  48.3 0.1 collective-permute-done.9.refs_4_
  48.4 3.6 %score.1 = f32[1,128]{1,0:T(1,128)S(1)} custom-call(f32[64,128]{1,0:T(8,128)S(1)} %get-tuple-element.17.refs_0_, bf16[1168,128]{1,0:T(8,128)(2,1)S(1)} %merge.5.refs_1_, bf16[1168,128]{1,0:T(8,128)(2,1)S(1)} %collective-permute-done.7.refs_2_, bf16[1168,128]{1,0:T(8,128)(2,1)S(1)} %collective-permute-done.8.refs_3_, ...), custom_call_target="tpu_custom_call" | custom-call | tf_op jit(solution)/shard_map/score/pallas_call | solution.py:339
  52.0 7.8 %collective-permute-start.10 = (f32[1,128]{1,0:T(1,128)S(1)}, f32[1,128]{1,0:T(1,128)S(1)}, u32[]{:S(2)}, u32[]{:S(2)}) collective-permute-start(f32[1,128]{1,0:T(1,128)S(1)} %score.1), channel_id=1, source_target_pairs={{0,1},{1,2},{2,3},{3,0},{4,5},{5,6},{6,7},{7,4},{8,9},{9,10},{10,1... | collective-permute-start | bytes 1544 | tf_op jit(solution)/shard_map/ppermute | solution.py:380
  59.9 0.0 collective-permute-start.11
  59.9 0.5 collective-permute-start.12
  60.4 0.2 collective-permute-done.10
  60.6 1.7 %collective-permute-done.11 = f32[1,128]{1,0:T(1,128)S(1)} collective-permute-done((f32[1,128]{1,0:T(1,128)S(1)}, f32[1,128]{1,0:T(1,128)S(1)}, u32[]{:S(2)}, u32[]{:S(2)}) %collective-permute-start.11) | collective-permute-done | bytes 544 | tf_op jit(solution)/shard_map/ppermute | solution.py:380
  62.3 0.6 collective-permute-done.12
  62.9 0.5 fusion.2
  (4 shorter events, 0.1 us)
Async XLA Ops:
  9.4 4.5 %collective-permute-start = (bf16[1024,128]{1,0:T(8,128)(2,1)S(1)}, bf16[1024,128]{1,0:T(8,128)(2,1)S(1)}, u32[]{:S(2)}, u32[]{:S(2)}) collective-permute-start(bf16[1024,128]{1,0:T(8,128)(2,1)S(1)} %get-tuple-element.13), channel_id=1, source_target_pairs={{0,1},{1,0},{2,3},{3,2},{4,5},{5,4},{6,7},{7,6},{8,9},{9,8},{10,11... | collective-permute-start | bytes 786440 | tf_op jit(solution)/shard_map/ppermute | solution.py:377
  13.9 4.8 %collective-permute-start.1 = (bf16[512,128]{1,0:T(8,128)(2,1)S(1)}, bf16[512,128]{1,0:T(8,128)(2,1)S(1)}, u32[]{:S(2)}, u32[]{:S(2)}) collective-permute-start(bf16[512,128]{1,0:T(8,128)(2,1)S(1)} %get-tuple-element.15), channel_id=1, source_target_pairs={{0,2},{1,3},{2,0},{3,1},{4,6},{5,7},{6,4},{7,5},{8,10},{9,11},{10,... | collective-permute-start | bytes 393224 | tf_op jit(solution)/shard_map/ppermute | solution.py:377
  19.3 4.5 %collective-permute-start.2 = (bf16[208,128]{1,0:T(8,128)(2,1)S(1)}, bf16[208,128]{1,0:T(8,128)(2,1)S(1)}, u32[]{:S(2)}, u32[]{:S(2)}) collective-permute-start(bf16[208,128]{1,0:T(8,128)(2,1)S(1)} %get-tuple-element.18.refs_0_), channel_id=1, source_target_pairs={{0,4},{4,0},{8,12},{12,8},{16,20},{20,16},{24,28},{28,24},{32,36},... | collective-permute-start | bytes 159752 | tf_op jit(solution)/shard_map/ppermute | solution.py:391
  23.9 5.7 %collective-permute-start.3 = (bf16[272,128]{1,0:T(8,128)(2,1)S(1)}, bf16[272,128]{1,0:T(8,128)(2,1)S(1)}, u32[]{:S(2)}, u32[]{:S(2)}) collective-permute-start(bf16[272,128]{1,0:T(8,128)(2,1)S(1)} %merge.3.refs_0_), channel_id=1, source_target_pairs={{0,12},{4,8},{8,4},{12,0},{16,28},{20,24},{24,20},{28,16},{32,44},... | collective-permute-start | bytes 208904 | tf_op jit(solution)/shard_map/ppermute | solution.py:391
  29.6 5.1 %collective-permute-start.4 = (bf16[400,128]{1,0:T(8,128)(2,1)S(1)}, bf16[400,128]{1,0:T(8,128)(2,1)S(1)}, u32[]{:S(2)}, u32[]{:S(2)}) collective-permute-start(bf16[400,128]{1,0:T(8,128)(2,1)S(1)} %merge.4.refs_0_), channel_id=1, source_target_pairs={{0,16},{1,65},{2,18},{3,67},{4,20},{5,69},{6,22},{7,71},{8,24},{9,... | collective-permute-start | bytes 307208 | tf_op jit(solution)/shard_map/ppermute | solution.py:373
  31.0 5.8 %collective-permute-start.5 = (bf16[400,128]{1,0:T(8,128)(2,1)S(1)}, bf16[400,128]{1,0:T(8,128)(2,1)S(1)}, u32[]{:S(2)}, u32[]{:S(2)}) collective-permute-start(bf16[400,128]{1,0:T(8,128)(2,1)S(1)} %merge.4.refs_0_), channel_id=1, source_target_pairs={{0,32},{1,129},{2,34},{3,131},{4,36},{5,133},{6,38},{7,135},{8,40}... | collective-permute-start | bytes 307208 | tf_op jit(solution)/shard_map/ppermute | solution.py:373
  33.6 3.8 %collective-permute-start.6 = (bf16[400,128]{1,0:T(8,128)(2,1)S(1)}, bf16[400,128]{1,0:T(8,128)(2,1)S(1)}, u32[]{:S(2)}, u32[]{:S(2)}) collective-permute-start(bf16[400,128]{1,0:T(8,128)(2,1)S(1)} %merge.4.refs_0_), channel_id=1, source_target_pairs={{0,48},{1,193},{2,50},{3,195},{4,52},{5,197},{6,54},{7,199},{8,56}... | collective-permute-start | bytes 307208 | tf_op jit(solution)/shard_map/ppermute | solution.py:373
  37.4 6.9 %collective-permute-start.7 = (bf16[1168,128]{1,0:T(8,128)(2,1)S(1)}, bf16[1168,128]{1,0:T(8,128)(2,1)S(1)}, u32[]{:S(2)}, u32[]{:S(2)}) collective-permute-start(bf16[1168,128]{1,0:T(8,128)(2,1)S(1)} %merge.5.refs_1_), channel_id=1, source_target_pairs={{0,64},{1,17},{2,66},{3,19},{4,68},{5,21},{6,70},{7,23},{8,72},{9,... | collective-permute-start | bytes 897032 | tf_op jit(solution)/shard_map/ppermute | solution.py:373
  38.5 9.8 %collective-permute-start.8 = (bf16[1168,128]{1,0:T(8,128)(2,1)S(1)}, bf16[1168,128]{1,0:T(8,128)(2,1)S(1)}, u32[]{:S(2)}, u32[]{:S(2)}) collective-permute-start(bf16[1168,128]{1,0:T(8,128)(2,1)S(1)} %merge.5.refs_1_), channel_id=1, source_target_pairs={{0,128},{1,33},{2,130},{3,35},{4,132},{5,37},{6,134},{7,39},{8,136... | collective-permute-start | bytes 897032 | tf_op jit(solution)/shard_map/ppermute | solution.py:373
  40.9 7.5 %collective-permute-start.9 = (bf16[1168,128]{1,0:T(8,128)(2,1)S(1)}, bf16[1168,128]{1,0:T(8,128)(2,1)S(1)}, u32[]{:S(2)}, u32[]{:S(2)}) collective-permute-start(bf16[1168,128]{1,0:T(8,128)(2,1)S(1)} %merge.5.refs_1_), channel_id=1, source_target_pairs={{0,192},{1,49},{2,194},{3,51},{4,196},{5,53},{6,198},{7,55},{8,200... | collective-permute-start | bytes 897032 | tf_op jit(solution)/shard_map/ppermute | solution.py:373
  52.0 8.5 %collective-permute-start.10 = (f32[1,128]{1,0:T(1,128)S(1)}, f32[1,128]{1,0:T(1,128)S(1)}, u32[]{:S(2)}, u32[]{:S(2)}) collective-permute-start(f32[1,128]{1,0:T(1,128)S(1)} %score.1), channel_id=1, source_target_pairs={{0,1},{1,2},{2,3},{3,0},{4,5},{5,6},{6,7},{7,4},{8,9},{9,10},{10,1... | collective-permute-start | bytes 1544 | tf_op jit(solution)/shard_map/ppermute | solution.py:380
  59.9 2.4 %collective-permute-start.11 = (f32[1,128]{1,0:T(1,128)S(1)}, f32[1,128]{1,0:T(1,128)S(1)}, u32[]{:S(2)}, u32[]{:S(2)}) collective-permute-start(f32[1,128]{1,0:T(1,128)S(1)} %score.1), channel_id=1, source_target_pairs={{0,2},{1,3},{2,0},{3,1},{4,6},{5,7},{6,4},{7,5},{8,10},{9,11},{10,... | collective-permute-start | bytes 1544 | tf_op jit(solution)/shard_map/ppermute | solution.py:380
  59.9 3.0 %collective-permute-start.12 = (f32[1,128]{1,0:T(1,128)S(1)}, f32[1,128]{1,0:T(1,128)S(1)}, u32[]{:S(2)}, u32[]{:S(2)}) collective-permute-start(f32[1,128]{1,0:T(1,128)S(1)} %score.1), channel_id=1, source_target_pairs={{0,3},{1,0},{2,1},{3,2},{4,7},{5,4},{6,5},{7,6},{8,11},{9,8},{10,9... | collective-permute-start | bytes 1544 | tf_op jit(solution)/shard_map/ppermute | solution.py:380
where the time goes:
time: 63.5 us; the launch traced here: 63.4 us
  starting transfers between devices  27.1 us (43%)
  waiting for transfers between devices  22 us (35%)
  Pallas kernels  13.7 us (22%)
    ppermute x6, starting transfers between devices, around(): lax.ppermute(value, ('dp', 'tensor'), ring(names, s, size))  9.72 us
    pallas_call x1, Pallas kernels, project(): pl.pallas_call(project_kernel, out_shape=[jax.ShapeDtypeStruct((2 * token...  9.38 us
    ppermute x6, waiting for transfers between devices, around(): lax.ppermute(value, ('dp', 'tensor'), ring(names, s, size))  9.08 us
    ppermute x3, starting transfers between devices, shifted(): lax.ppermute(value, 'tensor', [(i, (i + step) % 4) for i in range(4)])  8.31 us
    ppermute x2, waiting for transfers between devices, crossed(): return lax.ppermute(value, 'tensor', [(i, i ^ mask) for i in range(4)])  5.86 us
    ppermute x2, starting transfers between devices, body(): lax.ppermute(message, 'dp', flipped(RINGS['z'], mask, size))  5.61 us
    ppermute x2, waiting for transfers between devices, body(): lax.ppermute(message, 'dp', flipped(RINGS['z'], mask, size))  4.6 us
    pallas_call x1, Pallas kernels, score(): pl.pallas_call(lambda *refs: score_kernel(count, *refs), out_shape=jax.Sh...  3.64 us
  transfers between devices with their start and end apart: 13, of which 12 were waited for; matrix products, arithmetic and copies ran while one was open for 0% of the time, Pallas kernels for 0%

commit v1 on v0

--- a/solution.py
+++ b/solution.py
@@ -79,26 +79,23 @@
 
         @pl.when(c == 0)
         def _():
-            for k in range(1, 3):
+            for k in range(1, strips):
                 start(chunk_copies(k))
             arrive(weight_copies())
-
-        @pl.when((c > 0) & (c + 2 < strips))
-        def _():
-            start(chunk_copies(c + 2))
 
         at = pl.ds(pl.multiple_of(c * STRIP, STRIP), STRIP)
         g = hidden_buf[0, at, :].astype(jnp.float32)
         u = hidden_buf[1, at, :].astype(jnp.float32)
         e = hidden_buf[2, at, :].astype(jnp.float32)
-        th = jnp.tanh(0.5 * g)
-        p, q = 1.0 + th, 1.0 - th
-        a = g * p
-        gate_grad = ((e * u) * (p * (2.0 + g * q))).astype(jnp.bfloat16)
+        half = 0.5 * g
+        th = jnp.tanh(half)
+        p = 1.0 + th
+        a = half * p
+        gate_grad = ((e * u) * (p * (1.0 + (g - a)))).astype(jnp.bfloat16)
         up_grad = (e * a).astype(jnp.bfloat16)
         hid = (a * u).astype(jnp.bfloat16)
         for i, act in enumerate((gate_grad, up_grad, hid)):
-            sums[i, at, :RANK] = rows_dot(act, hidden_w[i]) * (0.25 if i == 0 else 0.5)
+            sums[i, at, :RANK] = rows_dot(act, hidden_w[i]) * (0.5 if i == 0 else 1.0)
         for i in range(2):
             sums[2 * i, at, RANK:] = rows_dot(side_buf[i, at, :], side_w[i])
 

time: 63.5 us -> 63.4 us (level)
  no operation moved by 1% of the time
where the time goes in v1:
time: 63.4 us; the launch traced here: 63.3 us
  starting transfers between devices  27.1 us (43%)
  waiting for transfers between devices  22 us (35%)
  Pallas kernels  13.7 us (22%)
    ppermute x6, starting transfers between devices, around(): lax.ppermute(value, ('dp', 'tensor'), ring(names, s, size))  9.71 us
    pallas_call x1, Pallas kernels, project(): pl.pallas_call(project_kernel, out_shape=[jax.ShapeDtypeStruct((2 * token...  9.32 us
    ppermute x6, waiting for transfers between devices, around(): lax.ppermute(value, ('dp', 'tensor'), ring(names, s, size))  9.08 us
    ppermute x3, starting transfers between devices, shifted(): lax.ppermute(value, 'tensor', [(i, (i + step) % 4) for i in range(4)])  8.31 us
    ppermute x2, waiting for transfers between devices, crossed(): return lax.ppermute(value, 'tensor', [(i, i ^ mask) for i in range(4)])  5.86 us
    ppermute x2, starting transfers between devices, body(): lax.ppermute(message, 'dp', flipped(RINGS['z'], mask, size))  5.62 us
    ppermute x2, waiting for transfers between devices, body(): lax.ppermute(message, 'dp', flipped(RINGS['z'], mask, size))  4.6 us
    pallas_call x1, Pallas kernels, score(): pl.pallas_call(lambda *refs: score_kernel(count, *refs), out_shape=jax.Sh...  3.64 us
  transfers between devices with their start and end apart: 13, of which 12 were waited for; matrix products, arithmetic and copies ran while one was open for 0% of the time, Pallas kernels for 0%

profile of v1, /device:TPU:1, one launch (start us, length us, event | category | flops | bytes accessed | tf_op | source)
XLA Modules:
  0.0 63.3 jit_solution(16357585825409913501)
XLA Ops:
  0.0 9.3 %project.1 = (f32[1024,128]{1,0:T(8,128)S(1)}, bf16[1024,128]{1,0:T(8,128)(2,1)S(1)}, bf16[64,128]{1,0:T(8,128)(2,1)S(1)}) custom-call(bf16[512,3584]{1,0:T(8,128)(2,1)} %gate_hbm.1, bf16[512,3584]{1,0:T(8,128)(2,1)} %up_hbm.1, bf16[512,3584]{1,0:T(8,128)(2,1)} %grad_hbm.1, bf16[512,1024]{1,0:T(8,128)(2,1)} %inputs_hbm.1, bf16[512,1024]{1,0:T(8,128)(2,1)} %outg_hbm.1, ...), custom_call_target="tpu_custom_call" | custom-call | flops 838860800 | bytes 17000000 | tf_op jit(solution)/shard_map/project/pallas_call | solution.py:124
  9.3 3.3 %collective-permute-start = (bf16[1024,128]{1,0:T(8,128)(2,1)S(1)}, bf16[1024,128]{1,0:T(8,128)(2,1)S(1)}, u32[]{:S(2)}, u32[]{:S(2)}) collective-permute-start(bf16[1024,128]{1,0:T(8,128)(2,1)S(1)} %get-tuple-element.13), channel_id=1, source_target_pairs={{0,1},{1,0},{2,3},{3,2},{4,5},{5,4},{6,7},{7,6},{8,9},{9,8},{10,11... | collective-permute-start | bytes 786440 | tf_op jit(solution)/shard_map/ppermute | solution.py:374
  12.7 1.2 %collective-permute-done.core_ref = bf16[1024,128]{1,0:T(8,128)(2,1)S(1)} collective-permute-done((bf16[1024,128]{1,0:T(8,128)(2,1)S(1)}, bf16[1024,128]{1,0:T(8,128)(2,1)S(1)}, u32[]{:S(2)}, u32[]{:S(2)}) %collective-permute-start) | collective-permute-done | bytes 262176 | tf_op jit(solution)/shard_map/ppermute | solution.py:374
  13.9 0.1 collective-permute-start.1
  14.0 4.7 %collective-permute-done.1.got_ref = bf16[512,128]{1,0:T(8,128)(2,1)S(1)} collective-permute-done((bf16[512,128]{1,0:T(8,128)(2,1)S(1)}, bf16[512,128]{1,0:T(8,128)(2,1)S(1)}, u32[]{:S(2)}, u32[]{:S(2)}) %collective-permute-start.1) | collective-permute-done | bytes 131104 | tf_op jit(solution)/shard_map/ppermute | solution.py:374
  18.7 0.6 gram.1
  19.2 1.7 %collective-permute-start.2 = (bf16[208,128]{1,0:T(8,128)(2,1)S(1)}, bf16[208,128]{1,0:T(8,128)(2,1)S(1)}, u32[]{:S(2)}, u32[]{:S(2)}) collective-permute-start(bf16[208,128]{1,0:T(8,128)(2,1)S(1)} %get-tuple-element.18.refs_0_), channel_id=1, source_target_pairs={{0,4},{4,0},{8,12},{12,8},{16,20},{20,16},{24,28},{28,24},{32,36},... | collective-permute-start | bytes 159752 | tf_op jit(solution)/shard_map/ppermute | solution.py:388
  21.0 2.8 %collective-permute-done.2.refs_1_ = bf16[208,128]{1,0:T(8,128)(2,1)S(1)} collective-permute-done((bf16[208,128]{1,0:T(8,128)(2,1)S(1)}, bf16[208,128]{1,0:T(8,128)(2,1)S(1)}, u32[]{:S(2)}, u32[]{:S(2)}) %collective-permute-start.2) | collective-permute-done | bytes 53280 | tf_op jit(solution)/shard_map/ppermute | solution.py:388
  23.8 3.9 %collective-permute-start.3 = (bf16[272,128]{1,0:T(8,128)(2,1)S(1)}, bf16[272,128]{1,0:T(8,128)(2,1)S(1)}, u32[]{:S(2)}, u32[]{:S(2)}) collective-permute-start(bf16[272,128]{1,0:T(8,128)(2,1)S(1)} %merge.3.refs_0_), channel_id=1, source_target_pairs={{0,12},{4,8},{8,4},{12,0},{16,28},{20,24},{24,20},{28,16},{32,44},... | collective-permute-start | bytes 208904 | tf_op jit(solution)/shard_map/ppermute | solution.py:388
  27.7 1.8 %collective-permute-done.3.refs_1_ = bf16[272,128]{1,0:T(8,128)(2,1)S(1)} collective-permute-done((bf16[272,128]{1,0:T(8,128)(2,1)S(1)}, bf16[272,128]{1,0:T(8,128)(2,1)S(1)}, u32[]{:S(2)}, u32[]{:S(2)}) %collective-permute-start.3) | collective-permute-done | bytes 69664 | tf_op jit(solution)/shard_map/ppermute | solution.py:388
  29.5 1.4 %collective-permute-start.4 = (bf16[400,128]{1,0:T(8,128)(2,1)S(1)}, bf16[400,128]{1,0:T(8,128)(2,1)S(1)}, u32[]{:S(2)}, u32[]{:S(2)}) collective-permute-start(bf16[400,128]{1,0:T(8,128)(2,1)S(1)} %merge.4.refs_0_), channel_id=1, source_target_pairs={{0,16},{1,65},{2,18},{3,67},{4,20},{5,69},{6,22},{7,71},{8,24},{9,... | collective-permute-start | bytes 307208 | tf_op jit(solution)/shard_map/ppermute | solution.py:370
  30.9 2.6 %collective-permute-start.5 = (bf16[400,128]{1,0:T(8,128)(2,1)S(1)}, bf16[400,128]{1,0:T(8,128)(2,1)S(1)}, u32[]{:S(2)}, u32[]{:S(2)}) collective-permute-start(bf16[400,128]{1,0:T(8,128)(2,1)S(1)} %merge.4.refs_0_), channel_id=1, source_target_pairs={{0,32},{1,129},{2,34},{3,131},{4,36},{5,133},{6,38},{7,135},{8,40}... | collective-permute-start | bytes 307208 | tf_op jit(solution)/shard_map/ppermute | solution.py:370
  33.5 1.1 %collective-permute-start.6 = (bf16[400,128]{1,0:T(8,128)(2,1)S(1)}, bf16[400,128]{1,0:T(8,128)(2,1)S(1)}, u32[]{:S(2)}, u32[]{:S(2)}) collective-permute-start(bf16[400,128]{1,0:T(8,128)(2,1)S(1)} %merge.4.refs_0_), channel_id=1, source_target_pairs={{0,48},{1,193},{2,50},{3,195},{4,52},{5,197},{6,54},{7,199},{8,56}... | collective-permute-start | bytes 307208 | tf_op jit(solution)/shard_map/ppermute | solution.py:370
  34.6 0.0 collective-permute-done.4.refs_1_
  34.6 2.1 %collective-permute-done.5.refs_2_ = bf16[400,128]{1,0:T(8,128)(2,1)S(1)} collective-permute-done((bf16[400,128]{1,0:T(8,128)(2,1)S(1)}, bf16[400,128]{1,0:T(8,128)(2,1)S(1)}, u32[]{:S(2)}, u32[]{:S(2)}) %collective-permute-start.5) | collective-permute-done | bytes 102432 | tf_op jit(solution)/shard_map/ppermute | solution.py:370
  36.6 0.7 %collective-permute-done.6.refs_3_ = bf16[400,128]{1,0:T(8,128)(2,1)S(1)} collective-permute-done((bf16[400,128]{1,0:T(8,128)(2,1)S(1)}, bf16[400,128]{1,0:T(8,128)(2,1)S(1)}, u32[]{:S(2)}, u32[]{:S(2)}) %collective-permute-start.6) | collective-permute-done | bytes 102432 | tf_op jit(solution)/shard_map/ppermute | solution.py:370
  37.3 1.0 %collective-permute-start.7 = (bf16[1168,128]{1,0:T(8,128)(2,1)S(1)}, bf16[1168,128]{1,0:T(8,128)(2,1)S(1)}, u32[]{:S(2)}, u32[]{:S(2)}) collective-permute-start(bf16[1168,128]{1,0:T(8,128)(2,1)S(1)} %merge.5.refs_1_), channel_id=1, source_target_pairs={{0,64},{1,17},{2,66},{3,19},{4,68},{5,21},{6,70},{7,23},{8,72},{9,... | collective-permute-start | bytes 897032 | tf_op jit(solution)/shard_map/ppermute | solution.py:370
  38.4 2.5 %collective-permute-start.8 = (bf16[1168,128]{1,0:T(8,128)(2,1)S(1)}, bf16[1168,128]{1,0:T(8,128)(2,1)S(1)}, u32[]{:S(2)}, u32[]{:S(2)}) collective-permute-start(bf16[1168,128]{1,0:T(8,128)(2,1)S(1)} %merge.5.refs_1_), channel_id=1, source_target_pairs={{0,128},{1,33},{2,130},{3,35},{4,132},{5,37},{6,134},{7,39},{8,136... | collective-permute-start | bytes 897032 | tf_op jit(solution)/shard_map/ppermute | solution.py:370
  40.8 1.2 %collective-permute-start.9 = (bf16[1168,128]{1,0:T(8,128)(2,1)S(1)}, bf16[1168,128]{1,0:T(8,128)(2,1)S(1)}, u32[]{:S(2)}, u32[]{:S(2)}) collective-permute-start(bf16[1168,128]{1,0:T(8,128)(2,1)S(1)} %merge.5.refs_1_), channel_id=1, source_target_pairs={{0,192},{1,49},{2,194},{3,51},{4,196},{5,53},{6,198},{7,55},{8,200... | collective-permute-start | bytes 897032 | tf_op jit(solution)/shard_map/ppermute | solution.py:370
  42.0 2.3 %collective-permute-done.7.refs_2_ = bf16[1168,128]{1,0:T(8,128)(2,1)S(1)} collective-permute-done((bf16[1168,128]{1,0:T(8,128)(2,1)S(1)}, bf16[1168,128]{1,0:T(8,128)(2,1)S(1)}, u32[]{:S(2)}, u32[]{:S(2)}) %collective-permute-start.7) | collective-permute-done | bytes 299040 | tf_op jit(solution)/shard_map/ppermute | solution.py:370
  44.3 3.9 %collective-permute-done.8.refs_3_ = bf16[1168,128]{1,0:T(8,128)(2,1)S(1)} collective-permute-done((bf16[1168,128]{1,0:T(8,128)(2,1)S(1)}, bf16[1168,128]{1,0:T(8,128)(2,1)S(1)}, u32[]{:S(2)}, u32[]{:S(2)}) %collective-permute-start.8) | collective-permute-done | bytes 299040 | tf_op jit(solution)/shard_map/ppermute | solution.py:370
  48.2 0.1 collective-permute-done.9.refs_4_
  48.3 3.6 %score.1 = f32[1,128]{1,0:T(1,128)S(1)} custom-call(f32[64,128]{1,0:T(8,128)S(1)} %get-tuple-element.17.refs_0_, bf16[1168,128]{1,0:T(8,128)(2,1)S(1)} %merge.5.refs_1_, bf16[1168,128]{1,0:T(8,128)(2,1)S(1)} %collective-permute-done.7.refs_2_, bf16[1168,128]{1,0:T(8,128)(2,1)S(1)} %collective-permute-done.8.refs_3_, ...), custom_call_target="tpu_custom_call" | custom-call | tf_op jit(solution)/shard_map/score/pallas_call | solution.py:336
  52.0 7.8 %collective-permute-start.10 = (f32[1,128]{1,0:T(1,128)S(1)}, f32[1,128]{1,0:T(1,128)S(1)}, u32[]{:S(2)}, u32[]{:S(2)}) collective-permute-start(f32[1,128]{1,0:T(1,128)S(1)} %score.1), channel_id=1, source_target_pairs={{0,1},{1,2},{2,3},{3,0},{4,5},{5,6},{6,7},{7,4},{8,9},{9,10},{10,1... | collective-permute-start | bytes 1544 | tf_op jit(solution)/shard_map/ppermute | solution.py:377
  59.8 0.0 collective-permute-start.11
  59.8 0.5 collective-permute-start.12
  60.3 0.2 collective-permute-done.10
  60.5 1.7 %collective-permute-done.11 = f32[1,128]{1,0:T(1,128)S(1)} collective-permute-done((f32[1,128]{1,0:T(1,128)S(1)}, f32[1,128]{1,0:T(1,128)S(1)}, u32[]{:S(2)}, u32[]{:S(2)}) %collective-permute-start.11) | collective-permute-done | bytes 544 | tf_op jit(solution)/shard_map/ppermute | solution.py:377
  62.2 0.6 collective-permute-done.12
  62.8 0.5 fusion.2
  (4 shorter events, 0.1 us)
Async XLA Ops:
  9.3 4.5 %collective-permute-start = (bf16[1024,128]{1,0:T(8,128)(2,1)S(1)}, bf16[1024,128]{1,0:T(8,128)(2,1)S(1)}, u32[]{:S(2)}, u32[]{:S(2)}) collective-permute-start(bf16[1024,128]{1,0:T(8,128)(2,1)S(1)} %get-tuple-element.13), channel_id=1, source_target_pairs={{0,1},{1,0},{2,3},{3,2},{4,5},{5,4},{6,7},{7,6},{8,9},{9,8},{10,11... | collective-permute-start | bytes 786440 | tf_op jit(solution)/shard_map/ppermute | solution.py:374
  13.9 4.8 %collective-permute-start.1 = (bf16[512,128]{1,0:T(8,128)(2,1)S(1)}, bf16[512,128]{1,0:T(8,128)(2,1)S(1)}, u32[]{:S(2)}, u32[]{:S(2)}) collective-permute-start(bf16[512,128]{1,0:T(8,128)(2,1)S(1)} %get-tuple-element.15), channel_id=1, source_target_pairs={{0,2},{1,3},{2,0},{3,1},{4,6},{5,7},{6,4},{7,5},{8,10},{9,11},{10,... | collective-permute-start | bytes 393224 | tf_op jit(solution)/shard_map/ppermute | solution.py:374
  19.2 4.5 %collective-permute-start.2 = (bf16[208,128]{1,0:T(8,128)(2,1)S(1)}, bf16[208,128]{1,0:T(8,128)(2,1)S(1)}, u32[]{:S(2)}, u32[]{:S(2)}) collective-permute-start(bf16[208,128]{1,0:T(8,128)(2,1)S(1)} %get-tuple-element.18.refs_0_), channel_id=1, source_target_pairs={{0,4},{4,0},{8,12},{12,8},{16,20},{20,16},{24,28},{28,24},{32,36},... | collective-permute-start | bytes 159752 | tf_op jit(solution)/shard_map/ppermute | solution.py:388
  23.8 5.7 %collective-permute-start.3 = (bf16[272,128]{1,0:T(8,128)(2,1)S(1)}, bf16[272,128]{1,0:T(8,128)(2,1)S(1)}, u32[]{:S(2)}, u32[]{:S(2)}) collective-permute-start(bf16[272,128]{1,0:T(8,128)(2,1)S(1)} %merge.3.refs_0_), channel_id=1, source_target_pairs={{0,12},{4,8},{8,4},{12,0},{16,28},{20,24},{24,20},{28,16},{32,44},... | collective-permute-start | bytes 208904 | tf_op jit(solution)/shard_map/ppermute | solution.py:388
  29.5 5.1 %collective-permute-start.4 = (bf16[400,128]{1,0:T(8,128)(2,1)S(1)}, bf16[400,128]{1,0:T(8,128)(2,1)S(1)}, u32[]{:S(2)}, u32[]{:S(2)}) collective-permute-start(bf16[400,128]{1,0:T(8,128)(2,1)S(1)} %merge.4.refs_0_), channel_id=1, source_target_pairs={{0,16},{1,65},{2,18},{3,67},{4,20},{5,69},{6,22},{7,71},{8,24},{9,... | collective-permute-start | bytes 307208 | tf_op jit(solution)/shard_map/ppermute | solution.py:370
  30.9 5.8 %collective-permute-start.5 = (bf16[400,128]{1,0:T(8,128)(2,1)S(1)}, bf16[400,128]{1,0:T(8,128)(2,1)S(1)}, u32[]{:S(2)}, u32[]{:S(2)}) collective-permute-start(bf16[400,128]{1,0:T(8,128)(2,1)S(1)} %merge.4.refs_0_), channel_id=1, source_target_pairs={{0,32},{1,129},{2,34},{3,131},{4,36},{5,133},{6,38},{7,135},{8,40}... | collective-permute-start | bytes 307208 | tf_op jit(solution)/shard_map/ppermute | solution.py:370
  33.5 3.8 %collective-permute-start.6 = (bf16[400,128]{1,0:T(8,128)(2,1)S(1)}, bf16[400,128]{1,0:T(8,128)(2,1)S(1)}, u32[]{:S(2)}, u32[]{:S(2)}) collective-permute-start(bf16[400,128]{1,0:T(8,128)(2,1)S(1)} %merge.4.refs_0_), channel_id=1, source_target_pairs={{0,48},{1,193},{2,50},{3,195},{4,52},{5,197},{6,54},{7,199},{8,56}... | collective-permute-start | bytes 307208 | tf_op jit(solution)/shard_map/ppermute | solution.py:370
  37.3 6.9 %collective-permute-start.7 = (bf16[1168,128]{1,0:T(8,128)(2,1)S(1)}, bf16[1168,128]{1,0:T(8,128)(2,1)S(1)}, u32[]{:S(2)}, u32[]{:S(2)}) collective-permute-start(bf16[1168,128]{1,0:T(8,128)(2,1)S(1)} %merge.5.refs_1_), channel_id=1, source_target_pairs={{0,64},{1,17},{2,66},{3,19},{4,68},{5,21},{6,70},{7,23},{8,72},{9,... | collective-permute-start | bytes 897032 | tf_op jit(solution)/shard_map/ppermute | solution.py:370
  38.4 9.8 %collective-permute-start.8 = (bf16[1168,128]{1,0:T(8,128)(2,1)S(1)}, bf16[1168,128]{1,0:T(8,128)(2,1)S(1)}, u32[]{:S(2)}, u32[]{:S(2)}) collective-permute-start(bf16[1168,128]{1,0:T(8,128)(2,1)S(1)} %merge.5.refs_1_), channel_id=1, source_target_pairs={{0,128},{1,33},{2,130},{3,35},{4,132},{5,37},{6,134},{7,39},{8,136... | collective-permute-start | bytes 897032 | tf_op jit(solution)/shard_map/ppermute | solution.py:370
  40.8 7.5 %collective-permute-start.9 = (bf16[1168,128]{1,0:T(8,128)(2,1)S(1)}, bf16[1168,128]{1,0:T(8,128)(2,1)S(1)}, u32[]{:S(2)}, u32[]{:S(2)}) collective-permute-start(bf16[1168,128]{1,0:T(8,128)(2,1)S(1)} %merge.5.refs_1_), channel_id=1, source_target_pairs={{0,192},{1,49},{2,194},{3,51},{4,196},{5,53},{6,198},{7,55},{8,200... | collective-permute-start | bytes 897032 | tf_op jit(solution)/shard_map/ppermute | solution.py:370
  52.0 8.5 %collective-permute-start.10 = (f32[1,128]{1,0:T(1,128)S(1)}, f32[1,128]{1,0:T(1,128)S(1)}, u32[]{:S(2)}, u32[]{:S(2)}) collective-permute-start(f32[1,128]{1,0:T(1,128)S(1)} %score.1), channel_id=1, source_target_pairs={{0,1},{1,2},{2,3},{3,0},{4,5},{5,6},{6,7},{7,4},{8,9},{9,10},{10,1... | collective-permute-start | bytes 1544 | tf_op jit(solution)/shard_map/ppermute | solution.py:377
  59.8 2.4 %collective-permute-start.11 = (f32[1,128]{1,0:T(1,128)S(1)}, f32[1,128]{1,0:T(1,128)S(1)}, u32[]{:S(2)}, u32[]{:S(2)}) collective-permute-start(f32[1,128]{1,0:T(1,128)S(1)} %score.1), channel_id=1, source_target_pairs={{0,2},{1,3},{2,0},{3,1},{4,6},{5,7},{6,4},{7,5},{8,10},{9,11},{10,... | collective-permute-start | bytes 1544 | tf_op jit(solution)/shard_map/ppermute | solution.py:377
  59.8 3.0 %collective-permute-start.12 = (f32[1,128]{1,0:T(1,128)S(1)}, f32[1,128]{1,0:T(1,128)S(1)}, u32[]{:S(2)}, u32[]{:S(2)}) collective-permute-start(f32[1,128]{1,0:T(1,128)S(1)} %score.1), channel_id=1, source_target_pairs={{0,3},{1,0},{2,1},{3,2},{4,7},{5,4},{6,5},{7,6},{8,11},{9,8},{10,9... | collective-permute-start | bytes 1544 | tf_op jit(solution)/shard_map/ppermute | solution.py:377
